TPU v7x, 32 devices: a whole 2x2x4 slice. The times are simulated.
32 devices in a mesh: pts: 32 (over z, y, x, core), rank: 1.
Axes of the slice: x: 2, y: 2, z: 4, core: 2. Of those that a mesh axis runs over, the one named last changes fastest.
Arguments:
- points: bfloat16 [32768, 256], P('pts', 'rank'), may hold values from -6 to 6
- prior: float32 [32768, 1024], P('pts', 'rank'), may hold values from -0.125 to 0.125
- first_pivots: int32 [256], replicated, may hold values from 0 to 32767, as said below
- second_pivots: int32 [256], replicated, may hold values from 0 to 32767, as said below
Outputs:
- first_columns: float32 [32768, 256], P('pts', 'rank')
- second_columns: float32 [32768, 256], P('pts', 'rank')
Inputs may be any that keep to these rules, and one draw needn't show every extreme that they name: `first_pivots`: the 256 entries are distinct, and none of them is in second_pivots. `second_pivots`: the 256 entries are distinct, and none of them is in first_pivots.
All inputs are finite; a program needn't handle non-finite values.
Results may differ from a plain program's by a relative error of at most 0.0003.
Values sent between devices are 32-bit elements; how exact they have to be, the bound alone decides.
A program may use at most 64 MiB of HBM per device.

v0:
```python
import jax
import jax.numpy as jnp
from jax import lax
from jax.sharding import PartitionSpec as P

NUGGET = 2.0


def contract(left_rows, right_rows, precise):
    dims = (((1,), (1,)), ((), ()))
    if precise:
        return lax.dot_general(
            left_rows,
            right_rows,
            dims,
            precision=lax.Precision.HIGHEST,
            preferred_element_type=jnp.float32,
        )
    return lax.dot_general(left_rows, right_rows, dims, preferred_element_type=jnp.float32)


def owned_rows(source, pivots, first_id):
    row_count = source.shape[0]
    local_index = pivots - first_id
    inside = (local_index >= 0) & (local_index < row_count)
    picked = jnp.take(source, jnp.clip(local_index, 0, row_count - 1), axis=0)
    return jnp.where(inside[:, None], picked.astype(jnp.float32), 0.0)


def square_norms(values):
    wide = values.astype(jnp.float32)
    return jnp.sum(wide * wide, axis=1)


def distance_part(left_rows, left_norms, right_rows, right_norms):
    return left_norms[:, None] + right_norms[None, :] - 2.0 * contract(left_rows, right_rows, False)


def inverse_factor(kernel_block):
    lower_factor = jnp.linalg.cholesky(kernel_block)
    identity = jnp.eye(kernel_block.shape[0], dtype=jnp.float32)
    return jax.scipy.linalg.solve_triangular(lower_factor, identity, lower=True)


def pivot_kernel(piv_x, piv_norms, piv_factor, feature_count):
    distance, product = lax.psum(
        (distance_part(piv_x, piv_norms, piv_x, piv_norms), contract(piv_factor, piv_factor, True)),
        "rank",
    )
    identity = jnp.eye(piv_x.shape[0], dtype=jnp.float32)
    return jnp.exp(-distance / feature_count) + NUGGET * identity - product


def kernel_panel(
    points, row_norms, left_parts, pivots, piv_x, piv_norms, right_parts, global_ids, feature_count
):
    distance_local = distance_part(points, row_norms, piv_x, piv_norms)
    product_local = contract(left_parts[0], right_parts[0], True)
    for left_rows, right_rows in zip(left_parts[1:], right_parts[1:]):
        product_local = product_local + contract(left_rows, right_rows, True)
    distance, product = lax.psum((distance_local, product_local), "rank")
    matches = (global_ids[:, None] == pivots[None, :]).astype(jnp.float32)
    return jnp.exp(-distance / feature_count) + NUGGET * matches - product


def own_columns(panel_block, inverse, col_start, col_count):
    return contract(panel_block, lax.dynamic_slice_in_dim(inverse, col_start, col_count, 0), True)


def per_device(points, prior, first_pivots, second_pivots):
    row_count = points.shape[0]
    first_id = lax.axis_index("pts") * row_count
    global_ids = first_id + lax.iota(jnp.int32, row_count)
    block = first_pivots.shape[0]
    col_count = block // lax.axis_size("rank")
    col_start = lax.axis_index("rank") * col_count
    feature_count = points.shape[1] * lax.axis_size("rank")
    row_norms = square_norms(points)
    gathered = lax.psum(
        (owned_rows(points, first_pivots, first_id), owned_rows(prior, first_pivots, first_id)),
        "pts",
    )
    first_x = gathered[0].astype(jnp.bfloat16)
    first_norms = square_norms(gathered[0])
    first_factor = gathered[1]
    first_kernel = pivot_kernel(first_x, first_norms, first_factor, feature_count)
    first_inverse = inverse_factor(first_kernel)
    first_panel = kernel_panel(
        points,
        row_norms,
        (prior,),
        first_pivots,
        first_x,
        first_norms,
        (first_factor,),
        global_ids,
        feature_count,
    )
    first_columns = own_columns(first_panel, first_inverse, col_start, col_count)
    later = lax.psum(
        (
            owned_rows(points, second_pivots, first_id),
            owned_rows(prior, second_pivots, first_id),
            owned_rows(first_columns, second_pivots, first_id),
        ),
        "pts",
    )
    second_x = later[0].astype(jnp.bfloat16)
    second_norms = square_norms(later[0])
    second_kernel = pivot_kernel(
        second_x, second_norms, jnp.concatenate([later[1], later[2]], axis=1), feature_count
    )
    right_parts = (later[1], later[2])
    second_inverse = inverse_factor(second_kernel)
    second_panel = kernel_panel(
        points,
        row_norms,
        (prior, first_columns),
        second_pivots,
        second_x,
        second_norms,
        right_parts,
        global_ids,
        feature_count,
    )
    second_columns = own_columns(second_panel, second_inverse, col_start, col_count)
    return (first_columns, second_columns)


def solution(mesh):
    return jax.shard_map(
        per_device,
        mesh=mesh,
        in_specs=(P("pts", "rank"), P("pts", "rank"), P(), P()),
        out_specs=(P("pts", "rank"), P("pts", "rank")),
        check_vma=False,
    )
```

profile of v0, /device:TPU:0, one launch (start us, length us, event | category | flops | bytes accessed | tf_op | source)
XLA Modules:
  0.0 442.4 jit_solution(17854518330767155222)
XLA Ops:
  8.0 3.8 gather_fusion.2
  16.2 3.8 gather_fusion.4
  21.5 127.7 %all-reduce.8.cloned.1.call-done = (f32[256,1024]{1,0:T(8,128)}, f32[256,256]{0,1:T(8,128)}) async-done(((f32[256,1024]{1,0:T(8,128)}, f32[256,256]{0,1:T(8,128)}), (f32[256,1024]{1,0:T(8,128)}, f32[256,256]{0,1:T(8,128)})) %all-reduce.8.cloned.1.call-update) | async-done | bytes 1310736 | tf_op jit(solution)/shard_map/psum | solution.py:79
  149.3 2.6 fusion.65
  151.9 5.7 %convolution_bitcast_fusion.1 = f32[1024,256]{1,0:T(8,128)S(1)} fusion(f32[256,1024]{1,0:T(8,128)} %get-tuple-element.41, f32[1024,1024]{1,0:T(8,128)} %param.12), kind=kOutput, calls=%fused_computation.27 | convolution fusion | flops 3221225472 | bytes 6291456 | tf_op jit(solution)/shard_map/dot_general | solution.py:12
  158.2 11.7 %cholesky.130 = f32[128,128]{1,0:T(8,128)S(1)} custom-call(f32[128,128]{1,0:T(8,128)S(1)} %cholesky.194), custom_call_target="Cholesky" | custom-call | tf_op jit(solution)/shard_map/jit(cholesky)/cholesky | solution.py:40
  169.9 9.8 %custom-call.13 = f32[1,128,128]{1,2,0:T(8,128)S(1)} custom-call(f32[1,128,128]{2,1,0:T(8,128)S(1)} %get-tuple-element.58), custom_call_target="InvertDiagBlocksLowerTriangular" | custom-call | tf_op jit(solution)/shard_map/jit(cholesky)/cholesky | solution.py:40
  180.2 11.7 %cholesky.147 = f32[128,128]{1,0:T(8,128)S(1)} custom-call(f32[128,128]{1,0:T(8,128)S(1)} %convolution_subtract_fusion.3), custom_call_target="Cholesky" | custom-call | tf_op jit(solution)/shard_map/jit(cholesky)/cholesky | solution.py:40
  194.7 4.0 while.4
  195.3 1.4 bitcast_dynamic-update-slice_fusion.4
  197.3 1.4 bitcast_dynamic-update-slice_fusion.4
  198.7 19.9 %custom-call.14 = f32[2,128,128]{1,2,0:T(8,128)S(1)} custom-call(f32[2,128,128]{2,1,0:T(8,128)S(1)} %get-tuple-element.20), custom_call_target="InvertDiagBlocksLowerTriangular" | custom-call | tf_op jit(solution)/shard_map/jit(_solve_triangular)/triangular_solve | solution.py:42
  223.1 132.1 %all-reduce.6.cloned.1.call-done = (f32[256,256]{0,1:T(8,128)}, f32[256,1024]{1,0:T(8,128)}, f32[256,256]{0,1:T(8,128)}) async-done(((f32[256,256]{0,1:T(8,128)}, f32[256,1024]{1,0:T(8,128)}, f32[256,256]{0,1:T(8,128)}), (f32[256,256]{0,1:T(8,128)}, f32[256,1024]{1,0:T(8,128)}, f32[256,256]{0,1:T(8,128)})) %all-reduce.6.cloned.1.call-update) | async-done | bytes 1572880 | tf_op jit(solution)/shard_map/psum | solution.py:100
  356.4 2.9 fusion.66
  360.4 2.9 fusion.15
  364.5 11.7 %cholesky.164 = f32[128,128]{1,0:T(8,128)S(1)} custom-call(f32[128,128]{1,0:T(8,128)S(1)} %cholesky.197), custom_call_target="Cholesky" | custom-call | tf_op jit(solution)/shard_map/jit(cholesky)/cholesky | solution.py:40
  376.2 9.8 %custom-call.15 = f32[1,128,128]{1,2,0:T(8,128)S(1)} custom-call(f32[1,128,128]{2,1,0:T(8,128)S(1)} %get-tuple-element.54), custom_call_target="InvertDiagBlocksLowerTriangular" | custom-call | tf_op jit(solution)/shard_map/jit(cholesky)/cholesky | solution.py:40
  388.2 11.9 %cholesky.181 = f32[128,128]{1,0:T(8,128)S(1)} custom-call(f32[128,128]{1,0:T(8,128)S(1)} %convolution_subtract_fusion.2), custom_call_target="Cholesky" | custom-call | tf_op jit(solution)/shard_map/jit(cholesky)/cholesky | solution.py:40
  402.7 3.8 while.5
  403.3 1.3 bitcast_dynamic-update-slice_fusion.5
  405.2 1.3 bitcast_dynamic-update-slice_fusion.5
  406.5 19.7 %custom-call.16 = f32[2,128,128]{1,2,0:T(8,128)S(1)} custom-call(f32[2,128,128]{2,1,0:T(8,128)S(1)} %get-tuple-element.21), custom_call_target="InvertDiagBlocksLowerTriangular" | custom-call | tf_op jit(solution)/shard_map/jit(_solve_triangular)/triangular_solve | solution.py:42
  427.2 5.3 %fusion.14 = f32[1024,256]{1,0:T(8,128)S(1)} fusion(f32[1024,256]{1,0:T(8,128)S(1)} %copy-done.3, f32[256,1024]{1,0:T(8,128)S(1)} %copy-done.2, f32[1024,1024]{1,0:T(8,128)} %param.12), kind=kOutput, calls=%fused_computation.26 | convolution fusion | flops 3221487616 | bytes 7340032 | tf_op jit(solution)/shard_map/dot_general | solution.py:12
  433.1 2.0 fusion.35
  (88 shorter events, 24.4 us)
Async XLA Ops:
  7.2 142.1 %all-reduce.8.cloned.1.call-start = ((), (), s32[]{:S(2)}) async-start(), calls=%async_computation.1 | async-start | bytes 2621440 | tf_op jit(solution)/shard_map/psum | solution.py:79
  7.9 3.8 copy-start.1
  15.0 340.3 %all-reduce.6.cloned.1.call-start = ((), (), s32[]{:S(2)}) async-start(), calls=%async_computation | async-start | bytes 3145728 | tf_op jit(solution)/shard_map/psum | solution.py:100
  149.2 8.4 %copy-start.5 = (f32[256,256]{0,1:T(8,128)S(1)}, f32[256,256]{0,1:T(8,128)}, u32[]{:S(2)}) copy-start(f32[256,256]{0,1:T(8,128)} %get-tuple-element.42) | copy-start | bytes 786436
  157.6 62.0 %copy-start.8 = (s32[256]{0:T(256)S(1)}, s32[256]{0:T(256)}, u32[]{:S(2)}) copy-start(s32[256]{0:T(256)} %param.13) | copy-start | bytes 3076
  221.2 139.2 %copy-start = (f32[1024,256]{1,0:T(8,128)}, f32[1024,256]{1,0:T(8,128)S(1)}, u32[]{:S(2)}) copy-start(f32[1024,256]{1,0:T(8,128)S(1)} %fusion.31) | copy-start | bytes 3145732
  355.3 8.0 %copy-start.6 = (f32[256,256]{0,1:T(8,128)S(1)}, f32[256,256]{0,1:T(8,128)}, u32[]{:S(2)}) copy-start(f32[256,256]{0,1:T(8,128)} %get-tuple-element.40) | copy-start | bytes 786436
  359.3 67.9 %copy-start.2 = (f32[256,1024]{1,0:T(8,128)S(1)}, f32[256,1024]{1,0:T(8,128)}, u32[]{:S(2)}) copy-start(f32[256,1024]{1,0:T(8,128)} %get-tuple-element.39) | copy-start | bytes 3145732
  360.4 66.8 %copy-start.3 = (f32[1024,256]{1,0:T(8,128)S(1)}, f32[1024,256]{1,0:T(8,128)}, u32[]{:S(2)}) copy-start(f32[1024,256]{1,0:T(8,128)} %fusion.66) | copy-start | bytes 3145732
  363.7 0.7 copy-start.4
  426.2 6.4 %copy-start.7 = (f32[256,256]{0,1:T(8,128)S(1)}, f32[256,256]{0,1:T(8,128)}, u32[]{:S(2)}) copy-start(f32[256,256]{0,1:T(8,128)} %get-tuple-element.40) | copy-start | bytes 786436
  426.2 6.4 %copy-start.9 = (s32[256]{0:T(256)S(1)}, s32[256]{0:T(256)}, u32[]{:S(2)}) copy-start(s32[256]{0:T(256)} %param.14) | copy-start | bytes 3076
Sparse Core Ops, SparseCore 0:
  15.1 134.1 all-reduce.7
  223.3 131.9 all-reduce.5
where the time goes:
time: 448 us; the launch traced here: 442 us
  waiting for transfers between devices  260 us (58%)
  other arithmetic  115 us (26%)
  matrix products  28.6 us (6%)
  local copies, waits for them, and re-layouts  21.1 us (5%)
  between operations  17.5 us (4%)
    psum x1, waiting for transfers between devices, per_device(): lax.psum((owned_rows(points, second_pivots, first_id), owned_rows(prior,...  132 us
    psum x1, waiting for transfers between devices, per_device(): lax.psum((owned_rows(points, first_pivots, first_id), owned_rows(prior, f...  128 us
    another operation x14, other arithmetic, inverse_factor(): lower_factor = jnp.linalg.cholesky(kernel_block)  69.4 us
    another operation x5, other arithmetic, inverse_factor(): return jax.scipy.linalg.solve_triangular(lower_factor, identity, lower=True)  39.6 us
    dot_general x7, matrix products, contract(): lax.dot_general(left_rows, right_rows, dims, precision=lax.Precision.HIGH...  22.4 us
    gather x8, local copies, waits for them, and re-layouts, owned_rows(): picked = jnp.take(source, jnp.clip(local_index, 0, row_count - 1), axis=0)  11.2 us
  transfers between devices with their start and end apart: 2, of which 2 were waited for; matrix products, arithmetic and copies ran while one was open for 1% of the time, Pallas kernels for 0%

commit v1 on v0

v1 whole, which is shorter than its diff:
```python
import functools

import jax
import jax.numpy as jnp
from jax import lax
from jax.experimental import pallas as pl
from jax.experimental.pallas import tpu as pltpu
from jax.sharding import PartitionSpec as P

NUGGET = 2.0
LANES = 128
GROUP = 8
MIB = 1 << 20


def contract(left_rows, right_rows, precision=None):
    return lax.dot_general(
        left_rows,
        right_rows,
        (((1,), (1,)), ((), ())),
        precision=precision,
        preferred_element_type=jnp.float32,
    )


def owned_rows(source, pivots, first_id):
    row_count = source.shape[0]
    local_index = pivots - first_id
    inside = (local_index >= 0) & (local_index < row_count)
    picked = jnp.take(source, jnp.clip(local_index, 0, row_count - 1), axis=0)
    return jnp.where(inside[:, None], picked.astype(jnp.float32), 0.0)


def square_norms(values):
    wide = values.astype(jnp.float32)
    return jnp.sum(wide * wide, axis=1)


def chain_plan(bits, columns):
    tiles = columns // LANES
    middle = list(range(1, bits - 1))
    ways = max(1, min(len(middle), 3, tiles))
    edges = [LANES * (tiles * way // ways) for way in range(ways + 1)]
    plan = []
    for way in range(ways):
        order = [0] + middle[way:] + middle[:way] + [bits - 1]
        plan.append((order, edges[way], edges[way + 1]))
    return plan


def exchange_kernel(bits, plan, mine_ref, sum_ref, work, landed, send_sem, recv_sem):
    me, rank = lax.axis_index("pts"), lax.axis_index("rank")
    rows = sum_ref.shape[0]
    half_of = [(me // (1 << b)) % 2 for b in range(bits)]
    partner_of = [me + (1 - 2 * half_of[b]) * (1 << b) for b in range(bits)]

    barrier = pltpu.get_barrier_semaphore()
    for b in range(bits):
        pl.semaphore_signal(
            barrier, inc=1, device_id=(partner_of[b], rank), device_id_type=pl.DeviceIdType.MESH
        )
    pl.semaphore_wait(barrier, bits)

    def copy(source, target, b, step, way):
        return pltpu.make_async_remote_copy(
            src_ref=source,
            dst_ref=target,
            send_sem=send_sem.at[step, way],
            recv_sem=recv_sem.at[step, way],
            device_id=(partner_of[b], rank),
            device_id_type=pl.DeviceIdType.MESH,
        )

    starts = [0 for _ in plan]
    running = [None for _ in plan]
    unit = rows >> bits

    def begin_halving(way, step):
        order, left, right = plan[way]
        b, size = order[step], rows >> (step + 1)
        offset = rows - (rows >> step)
        away = pl.multiple_of(starts[way] + (1 - half_of[b]) * size, unit)
        source = work if step else mine_ref
        running[way] = copy(
            source.at[pl.ds(away, size), pl.ds(left, right - left)],
            landed.at[pl.ds(offset, size), pl.ds(left, right - left)],
            b, step, way,
        )
        running[way].start()

    def end_halving(way, step):
        order, left, right = plan[way]
        b, size = order[step], rows >> (step + 1)
        offset = rows - (rows >> step)
        running[way].wait()
        starts[way] = starts[way] + half_of[b] * size
        keep = pl.ds(pl.multiple_of(starts[way], unit), size)
        source = work if step else mine_ref
        target = work if step < bits - 1 else sum_ref
        target[keep, left:right] = source[keep, left:right] + landed[offset:offset + size, left:right]

    def begin_doubling(way, step):
        order, left, right = plan[way]
        b, size = order[step], rows >> (step + 1)
        block = sum_ref.at[pl.ds(pl.multiple_of(starts[way], unit), size), pl.ds(left, right - left)]
        running[way] = copy(block, block, b, 2 * bits - 1 - step, way)
        running[way].start()

    def end_doubling(way, step):
        order, left, right = plan[way]
        b, size = order[step], rows >> (step + 1)
        running[way].wait()
        starts[way] = starts[way] - half_of[b] * size

    ways = range(len(plan))
    for way in ways:
        begin_halving(way, 0)
    for step in range(bits):
        for way in ways:
            end_halving(way, step)
            if step < bits - 1:
                begin_halving(way, step + 1)
            else:
                begin_doubling(way, step)
    for step in reversed(range(bits)):
        for way in ways:
            end_doubling(way, step)
            if step > 0:
                begin_doubling(way, step - 1)


def sum_over_points(mine):
    count = lax.axis_size("pts")
    rows, columns = mine.shape
    bits = count.bit_length() - 1
    if count != 1 << bits or bits < 3 or rows % (8 * count) or columns % LANES:
        return lax.psum(mine, "pts")
    plan = chain_plan(bits, columns)
    return pl.pallas_call(
        functools.partial(exchange_kernel, bits, plan),
        out_shape=jax.ShapeDtypeStruct(mine.shape, jnp.float32),
        in_specs=[pl.BlockSpec(memory_space=pltpu.VMEM)],
        out_specs=pl.BlockSpec(memory_space=pltpu.VMEM),
        scratch_shapes=[
            pltpu.VMEM((rows, columns), jnp.float32),
            pltpu.VMEM((rows, columns), jnp.float32),
            pltpu.SemaphoreType.DMA((2 * bits, len(plan))),
            pltpu.SemaphoreType.DMA((2 * bits, len(plan))),
        ],
        compiler_params=pltpu.CompilerParams(
            collective_id=0, has_side_effects=True, vmem_limit_bytes=24 * MIB
        ),
    )(mine)


def invert_diagonal(tiles):
    count = len(tiles)
    tiles = list(tiles)
    sub = lax.broadcasted_iota(jnp.int32, (GROUP, LANES), 0)
    lane = lax.broadcasted_iota(jnp.int32, (GROUP, LANES), 1)
    result = []
    for g in range(count):
        base = g * GROUP
        rows = tiles[g]
        cols = [jnp.broadcast_to(rows[:, base + k:base + k + 1], (GROUP, LANES)) for k in range(GROUP)]
        in_group = (lane >= base) & (lane < base + GROUP)
        rows = jnp.where(in_group, jnp.where(lane == sub + base, 1.0, 0.0), rows)
        scale = jnp.zeros((GROUP, LANES), jnp.float32)
        for k in range(GROUP):
            inv = 1.0 / jnp.broadcast_to(cols[k][k:k + 1, :], (GROUP, LANES))
            scale = jnp.where(sub == k, inv, scale)
            if k < GROUP - 1:
                mult = jnp.where(sub > k, cols[k] * inv, 0.0)
                for j in range(k + 1, GROUP):
                    cols[j] = cols[j] - mult * jnp.broadcast_to(cols[j][k:k + 1, :], (GROUP, LANES))
                rows = rows - mult * jnp.broadcast_to(rows[k:k + 1, :], (GROUP, LANES))
        result.append(jnp.where(lane <= sub + base, rows * jnp.sqrt(scale), 0.0))
        if g < count - 1:
            across = jnp.transpose(rows * scale)
            spread = [jnp.broadcast_to(rows[k:k + 1, :], (GROUP, LANES)) for k in range(GROUP)]
            for i in range(g + 1, count):
                part = across[i * GROUP:(i + 1) * GROUP, :]
                tile = jnp.where(in_group, 0.0, tiles[i])
                for k in range(GROUP):
                    tile = tile - jnp.broadcast_to(part[:, k:k + 1], (GROUP, LANES)) * spread[k]
                tiles[i] = tile
    return result


def inverse_kernel(a_ref, w_ref, work):
    size = a_ref.shape[0]
    blocks = size // LANES
    exact = lax.Precision.HIGHEST
    work[...] = a_ref[...]
    for b in range(blocks):
        low, high = b * LANES, (b + 1) * LANES
        tiles = [work[low + t * GROUP:low + (t + 1) * GROUP, low:high] for t in range(LANES // GROUP)]
        inverse = jnp.concatenate(invert_diagonal(tiles), axis=0)
        parts = []
        if b > 0:
            parts.append(jnp.dot(inverse, work[low:high, :low], precision=exact, preferred_element_type=jnp.float32))
        parts.append(inverse)
        left = jnp.concatenate(parts, axis=1)
        w_ref[low:high, :high] = left
        if high < size:
            w_ref[low:high, high:] = jnp.zeros((LANES, size - high), jnp.float32)
            right = jnp.dot(inverse, work[low:high, high:], precision=exact, preferred_element_type=jnp.float32)
            work[high:, low:high] = jnp.zeros((size - high, LANES), jnp.float32)
            work[high:, :] -= lax.dot_general(
                right,
                jnp.concatenate([left, right], axis=1),
                (((0,), (0,)), ((), ())),
                precision=exact,
                preferred_element_type=jnp.float32,
            )


def inverse_factor(kernel_block):
    size = kernel_block.shape[0]
    return pl.pallas_call(
        inverse_kernel,
        out_shape=jax.ShapeDtypeStruct((size, size), jnp.float32),
        in_specs=[pl.BlockSpec(memory_space=pltpu.VMEM)],
        out_specs=pl.BlockSpec(memory_space=pltpu.VMEM),
        scratch_shapes=[pltpu.VMEM((size, size), jnp.float32)],
        compiler_params=pltpu.CompilerParams(vmem_limit_bytes=24 * MIB),
    )(kernel_block)


def per_device(points, prior, first_pivots, second_pivots):
    row_count, width = points.shape
    ranks = lax.axis_size("rank")
    block = first_pivots.shape[0]
    pivots = jnp.concatenate([first_pivots, second_pivots])
    first_id = lax.axis_index("pts") * row_count
    global_ids = first_id + lax.iota(jnp.int32, row_count)
    feature_count = width * ranks
    mine = jnp.concatenate(
        [owned_rows(prior, pivots, first_id), owned_rows(points, pivots, first_id)], axis=1
    )
    gathered = sum_over_points(mine)
    piv_factor, piv_wide = gathered[:, :-width], gathered[:, -width:]
    piv_x = piv_wide.astype(jnp.bfloat16)
    piv_norms = square_norms(piv_wide)
    row_norms = square_norms(points)

    def combine(rows, norms, factor, matches):
        distance = norms[:, None] + piv_norms[None, :] - 2.0 * contract(rows, piv_x)
        product = contract(factor, piv_factor, lax.Precision.HIGH)
        if ranks > 1:
            distance, product = lax.psum((distance, product), "rank")
        return jnp.exp(-distance / feature_count) + NUGGET * matches.astype(jnp.float32) - product

    kernel_block = combine(piv_x, piv_norms, piv_factor, jnp.eye(2 * block, dtype=jnp.float32))
    inverse = inverse_factor(kernel_block)
    panel = combine(points, row_norms, prior, global_ids[:, None] == pivots[None, :])
    own = block // ranks
    start = lax.axis_index("rank") * own
    first_inverse = lax.dynamic_slice_in_dim(inverse[:block, :block], start, own, 0)
    second_inverse = lax.dynamic_slice_in_dim(inverse[block:], start, own, 0)
    first_columns = contract(panel[:, :block], first_inverse, lax.Precision.HIGH)
    second_columns = contract(panel, second_inverse, lax.Precision.HIGH)
    return (first_columns, second_columns)


def solution(mesh):
    return jax.shard_map(
        per_device,
        mesh=mesh,
        in_specs=(P("pts", "rank"), P("pts", "rank"), P(), P()),
        out_specs=(P("pts", "rank"), P("pts", "rank")),
        check_vma=False,
    )
```

time: 448 us -> 92.9 us (0.21); the launches traced: 442 us -> 92.7 us
  waiting for transfers between devices: 260 us -> 0 us
  other arithmetic: 115 us -> 1.81 us
  Pallas kernels: 0 us -> 70.5 us
  matrix products: 28.6 us -> 11.8 us
  between operations: 17.5 us -> 0.81 us
  local copies, waits for them, and re-layouts: 21.1 us -> 7.73 us
    psum x2 -> x0, waiting for transfers between devices: 260 us -> none  [the longest x1 132 us: per_device(): lax.psum((owned_rows(points, second_pivots, first_id), owned_rows(prior,...]
    another operation x19 -> x0, other arithmetic: 109 us -> none  [the longest x14 69.4 us: inverse_factor(): lower_factor = jnp.linalg.cholesky(kernel_block)]
    pallas_call x0 -> x2, Pallas kernels: none -> 70.5 us  [the longest x1 44.9 us: sum_over_points(): pl.pallas_call(functools.partial(exchange_kernel, bits, plan), out_shape=...]
    dot_general x11 -> x6, matrix products: 24 us -> 11.8 us  [contract(): lax.dot_general(left_rows, right_rows, (((1,), (1,)), ((), ())), precisio...]
    another operation x19 -> x0, local copies, waits for them, and re-layouts: 7.8 us -> none  [the longest x15 7.76 us: inverse_factor(): return jax.scipy.linalg.solve_triangular(lower_factor, identity, lower=True)]
    another operation x10 -> x0, matrix products: 4.64 us -> none  [the longest x4 2.62 us: inverse_factor(): lower_factor = jnp.linalg.cholesky(kernel_block)]
    gather x8 -> x2, local copies, waits for them, and re-layouts: 11.2 us -> 7.68 us  [owned_rows(): picked = jnp.take(source, jnp.clip(local_index, 0, row_count - 1), axis=0)]
  transfers between devices with their start and end apart: 2 -> 0, of which waited for: 2 -> 0; matrix products, arithmetic and copies ran while one was open for 1% -> 0% of each run, Pallas kernels for 0% -> 0%
where the time goes in v1:
time: 92.9 us; the launch traced here: 92.7 us
  Pallas kernels  70.5 us (76%)
  matrix products  11.8 us (13%)
  local copies, waits for them, and re-layouts  7.73 us (8%)
  other arithmetic  1.81 us (2%)
    pallas_call x1, Pallas kernels, sum_over_points(): pl.pallas_call(functools.partial(exchange_kernel, bits, plan), out_shape=...  44.9 us
    pallas_call x1, Pallas kernels, inverse_factor(): pl.pallas_call(inverse_kernel, out_shape=jax.ShapeDtypeStruct((size, size...  25.6 us
    dot_general x6, matrix products, contract(): lax.dot_general(left_rows, right_rows, (((1,), (1,)), ((), ())), precisio...  11.8 us
    gather x2, local copies, waits for them, and re-layouts, owned_rows(): picked = jnp.take(source, jnp.clip(local_index, 0, row_count - 1), axis=0)  7.68 us

profile of v1, /device:TPU:0, one launch (start us, length us, event | category | flops | bytes accessed | tf_op | source)
XLA Modules:
  0.0 92.7 jit_solution(14891235760446318513)
XLA Ops:
  0.6 0.0 copy-start.3
  0.6 0.0 copy-start.2
  0.7 0.7 compare_select_fusion
  1.4 2.7 %gather_fusion.1 = bf16[512,256]{1,0:T(8,128)(2,1)S(1)} fusion(bf16[1024,256]{1,0:T(8,128)(2,1)} %param.4, s32[1024]{0:T(1024)S(1)} %pad_clamp_fusion), kind=kCustom, calls=%fused_computation.1 | custom fusion | bytes 526336 | tf_op jit(solution)/shard_map/jit(_take)/gather | solution.py:30
  4.1 0.0 copy-done.2
  4.1 0.0 copy-done.3
  4.2 0.2 convert_select_fusion
  4.4 5.0 %gather_fusion = f32[512,1024]{1,0:T(8,128)S(1)} fusion(f32[1024,1024]{1,0:T(8,128)} %param.5, s32[1024]{0:T(1024)S(1)} %pad_clamp_fusion), kind=kCustom, calls=%fused_computation | custom fusion | bytes 4196352 | tf_op jit(solution)/shard_map/jit(_take)/gather | solution.py:30
  9.4 0.3 select_select_fusion
  9.7 0.2 pad_maximum_fusion.mine_ref
  9.9 0.0 copy-start
  9.9 44.9 %shard_map.59 = f32[512,1280]{1,0:T(8,128)S(1)} custom-call(f32[512,1280]{1,0:T(8,128)S(1)} %pad_maximum_fusion.mine_ref), custom_call_target="tpu_custom_call" | custom-call | tf_op jit(solution)/shard_map/pallas_call | solution.py:139
  54.8 0.0 copy-done
  54.8 0.0 copy-start.1
  54.8 3.7 %fusion.6 = f32[512,1024]{1,0:T(8,128)S(1)} fusion(f32[1024,1024]{1,0:T(8,128)S(1)} %copy-done, f32[512,1280]{1,0:T(8,128)S(1)} %shard_map.59), kind=kOutput, calls=%fused_computation.12 | convolution fusion | flops 3221225472 | bytes 8388608 | tf_op jit(solution)/shard_map/dot_general | solution.py:17
  58.5 0.1 multiply_reduce_fusion.1
  58.7 0.0 copy-done.1
  58.7 0.2 multiply_reduce_fusion
  58.9 0.9 bitcast_subtract_fusion
  59.8 0.4 fusion.15
  60.3 2.0 %fusion.8.a_ref = f32[512,512]{1,0:T(8,128)S(1)} fusion(f32[512,512]{1,0:T(8,128)S(1)} %fusion.15, f32[512,1280]{1,0:T(8,128)S(1)} %shard_map.59), kind=kOutput, calls=%fused_computation.14 | convolution fusion | flops 1610874880 | bytes 4194304 | tf_op jit(solution)/shard_map/dot_general | solution.py:17
  62.2 25.6 %shard_map.60 = f32[512,512]{1,0:T(8,128)S(1)} custom-call(f32[512,512]{1,0:T(8,128)S(1)} %fusion.8.a_ref), custom_call_target="tpu_custom_call" | custom-call | tf_op jit(solution)/shard_map/pallas_call | solution.py:220
  87.9 2.0 %fusion.16 = f32[1024,256]{1,0:T(8,128)} fusion(f32[1024,512]{0,1:T(8,128)S(1)} %bitcast_subtract_fusion, f32[512,512]{1,0:T(8,128)S(1)} %shard_map.60), kind=kOutput, calls=%fused_computation.21 | convolution fusion | flops 402653184 | bytes 2359296 | tf_op jit(solution)/shard_map/dot_general | solution.py:17
  89.8 2.8 %fusion.18 = f32[1024,256]{1,0:T(8,128)} fusion(f32[1024,512]{0,1:T(8,128)S(1)} %bitcast_subtract_fusion, f32[512,512]{1,0:T(8,128)S(1)} %shard_map.60), kind=kOutput, calls=%fused_computation.25 | convolution fusion | flops 805306368 | bytes 3670016 | tf_op jit(solution)/shard_map/dot_general | solution.py:17
  (6 shorter events, 0.1 us)
Async XLA Ops:
  0.6 3.5 %copy-start.3 = (s32[256]{0:T(256)S(1)}, s32[256]{0:T(256)}, u32[]{:S(2)}) copy-start(s32[256]{0:T(256)} %param.7) | copy-start | bytes 3076
  0.6 3.5 %copy-start.2 = (s32[256]{0:T(256)S(1)}, s32[256]{0:T(256)}, u32[]{:S(2)}) copy-start(s32[256]{0:T(256)} %param.6) | copy-start | bytes 3076
  9.9 44.9 %copy-start = (f32[1024,1024]{1,0:T(8,128)S(1)}, f32[1024,1024]{1,0:T(8,128)}, u32[]{:S(2)}) copy-start(f32[1024,1024]{1,0:T(8,128)} %param.5) | copy-start | bytes 12582916
  54.8 3.9 %copy-start.1 = (bf16[1024,256]{1,0:T(8,128)(2,1)S(1)}, bf16[1024,256]{1,0:T(8,128)(2,1)}, u32[]{:S(2)}) copy-start(bf16[1024,256]{1,0:T(8,128)(2,1)} %param.4) | copy-start | bytes 1572868

commit v2 on v1

--- a/solution.py
+++ b/solution.py
@@ -23,12 +23,52 @@
     )
 
 
-def owned_rows(source, pivots, first_id):
-    row_count = source.shape[0]
-    local_index = pivots - first_id
-    inside = (local_index >= 0) & (local_index < row_count)
-    picked = jnp.take(source, jnp.clip(local_index, 0, row_count - 1), axis=0)
-    return jnp.where(inside[:, None], picked.astype(jnp.float32), 0.0)
+ROW_TILE = 16
+
+
+def owned_kernel(pivots_ref, points_ref, prior_ref, mine_ref):
+    row_count, width = points_ref.shape
+    first_id = lax.axis_index("pts") * row_count
+    mine_ref[...] = jnp.zeros_like(mine_ref)
+
+    def group(g, carry):
+        local = [pivots_ref[g * GROUP + k] - first_id for k in range(GROUP)]
+        inside = [(index >= 0) & (index < row_count) for index in local]
+        some = functools.reduce(jnp.logical_or, inside)
+
+        @pl.when(some)
+        def _():
+            for k in range(GROUP):
+
+                @pl.when(inside[k])
+                def _():
+                    target = pl.ds(g * GROUP + k, 1)
+                    factor = prior_ref[pl.ds(local[k], 1), :]
+                    start = pl.multiple_of((local[k] // ROW_TILE) * ROW_TILE, ROW_TILE)
+                    near = points_ref[pl.ds(start, ROW_TILE), :].astype(jnp.float32)
+                    place = lax.broadcasted_iota(jnp.int32, near.shape, 0)
+                    picked = jnp.where(place == local[k] - start, near, 0.0)
+                    features = jnp.sum(picked, axis=0, keepdims=True)
+                    mine_ref[target, :] = jnp.concatenate([factor, features], axis=1)
+
+        return carry
+
+    lax.fori_loop(0, mine_ref.shape[0] // GROUP, group, 0)
+
+
+def owned_rows(points, prior, pivots):
+    columns = prior.shape[1] + points.shape[1]
+    return pl.pallas_call(
+        owned_kernel,
+        out_shape=jax.ShapeDtypeStruct((pivots.shape[0], columns), jnp.float32),
+        in_specs=[
+            pl.BlockSpec(memory_space=pltpu.SMEM),
+            pl.BlockSpec(memory_space=pltpu.VMEM),
+            pl.BlockSpec(memory_space=pltpu.VMEM),
+        ],
+        out_specs=pl.BlockSpec(memory_space=pltpu.VMEM),
+        compiler_params=pltpu.CompilerParams(vmem_limit_bytes=24 * MIB),
+    )(pivots, points, prior)
 
 
 def square_norms(values):
@@ -166,19 +206,35 @@
         in_group = (lane >= base) & (lane < base + GROUP)
         rows = jnp.where(in_group, jnp.where(lane == sub + base, 1.0, 0.0), rows)
         scale = jnp.zeros((GROUP, LANES), jnp.float32)
+        ahead = g < count - 1
+        if ahead:
+            nearby = tiles[g + 1]
+            below = [
+                jnp.broadcast_to(nearby[:, base + k:base + k + 1], (GROUP, LANES)) for k in range(GROUP)
+            ]
+            nearby = jnp.where(in_group, 0.0, nearby)
         for k in range(GROUP):
             inv = 1.0 / jnp.broadcast_to(cols[k][k:k + 1, :], (GROUP, LANES))
             scale = jnp.where(sub == k, inv, scale)
+            pivot_row = jnp.broadcast_to(rows[k:k + 1, :], (GROUP, LANES))
+            heads = [jnp.broadcast_to(cols[j][k:k + 1, :], (GROUP, LANES)) for j in range(k + 1, GROUP)]
             if k < GROUP - 1:
                 mult = jnp.where(sub > k, cols[k] * inv, 0.0)
                 for j in range(k + 1, GROUP):
-                    cols[j] = cols[j] - mult * jnp.broadcast_to(cols[j][k:k + 1, :], (GROUP, LANES))
-                rows = rows - mult * jnp.broadcast_to(rows[k:k + 1, :], (GROUP, LANES))
+                    cols[j] = cols[j] - mult * heads[j - k - 1]
+                rows = rows - mult * pivot_row
+            if ahead:
+                mult = below[k] * inv
+                for j in range(k + 1, GROUP):
+                    below[j] = below[j] - mult * heads[j - k - 1]
+                nearby = nearby - mult * pivot_row
         result.append(jnp.where(lane <= sub + base, rows * jnp.sqrt(scale), 0.0))
-        if g < count - 1:
+        if ahead:
+            tiles[g + 1] = nearby
+        if g < count - 2:
             across = jnp.transpose(rows * scale)
             spread = [jnp.broadcast_to(rows[k:k + 1, :], (GROUP, LANES)) for k in range(GROUP)]
-            for i in range(g + 1, count):
+            for i in range(g + 2, count):
                 part = across[i * GROUP:(i + 1) * GROUP, :]
                 tile = jnp.where(in_group, 0.0, tiles[i])
                 for k in range(GROUP):
@@ -235,9 +291,7 @@
     first_id = lax.axis_index("pts") * row_count
     global_ids = first_id + lax.iota(jnp.int32, row_count)
     feature_count = width * ranks
-    mine = jnp.concatenate(
-        [owned_rows(prior, pivots, first_id), owned_rows(points, pivots, first_id)], axis=1
-    )
+    mine = owned_rows(points, prior, pivots)
     gathered = sum_over_points(mine)
     piv_factor, piv_wide = gathered[:, :-width], gathered[:, -width:]
     piv_x = piv_wide.astype(jnp.bfloat16)

time: 92.9 us -> 91.7 us (0.987)
  local copies, waits for them, and re-layouts: 7.73 us -> 4.62 us
  matrix products: 11.8 us -> 14.6 us
  other arithmetic: 1.81 us -> 0.36 us
  Pallas kernels: 70.5 us -> 71.7 us
    gather x2 -> x0, local copies, waits for them, and re-layouts: 7.68 us -> none  [owned_rows(): picked = jnp.take(source, jnp.clip(local_index, 0, row_count - 1), axis=0)]
    unnamed x9, local copies, waits for them, and re-layouts: 0.04 us -> 3.93 us
    pallas_call x0 -> x1, Pallas kernels: none -> 3.82 us  [owned_rows(): pl.pallas_call(owned_kernel, out_shape=jax.ShapeDtypeStruct((pivots.shape...]
    pallas_call x1, Pallas kernels: 25.6 us -> 22 us  [inverse_factor(): pl.pallas_call(inverse_kernel, out_shape=jax.ShapeDtypeStruct((size, size...]
    dot_general x6, matrix products: 11.8 us -> 14.6 us  [contract(): lax.dot_general(left_rows, right_rows, (((1,), (1,)), ((), ())), precisio...]
    select_n x3 -> x0, other arithmetic: 1.23 us -> none  [the longest x1 0.75 us: owned_rows(): picked = jnp.take(source, jnp.clip(local_index, 0, row_count - 1), axis=0)]
where the time goes in v2:
time: 91.7 us; the launch traced here: 91.9 us
  Pallas kernels  71.7 us (78%)
  matrix products  14.6 us (16%)
  local copies, waits for them, and re-layouts  4.62 us (5%)
    pallas_call x1, Pallas kernels, sum_over_points(): pl.pallas_call(functools.partial(exchange_kernel, bits, plan), out_shape=...  45.8 us
    pallas_call x1, Pallas kernels, inverse_factor(): pl.pallas_call(inverse_kernel, out_shape=jax.ShapeDtypeStruct((size, size...  22 us
    dot_general x6, matrix products, contract(): lax.dot_general(left_rows, right_rows, (((1,), (1,)), ((), ())), precisio...  14.6 us
    unnamed x9, local copies, waits for them, and re-layouts  3.93 us
    pallas_call x1, Pallas kernels, owned_rows(): pl.pallas_call(owned_kernel, out_shape=jax.ShapeDtypeStruct((pivots.shape...  3.82 us

profile of v2, /device:TPU:0, one launch (start us, length us, event | category | flops | bytes accessed | tf_op | source)
XLA Modules:
  0.0 91.9 jit_solution(16712925108739326229)
XLA Ops:
  0.6 0.7 constant_dynamic-update-slice_fusion.1
  1.3 0.7 constant_dynamic-update-slice_fusion.pivots_ref
  2.0 0.0 copy-start
  2.0 2.2 %copy-done = f32[1024,1024]{1,0:T(8,128)S(1)} copy-done((f32[1024,1024]{1,0:T(8,128)S(1)}, f32[1024,1024]{1,0:T(8,128)}, u32[]{:S(2)}) %copy-start) | copy-done | bytes 4194328
  4.2 0.0 copy-start.2
  4.2 1.0 %copy-done.2 = bf16[1024,256]{1,0:T(8,128)(2,1)S(1)} copy-done((bf16[1024,256]{1,0:T(8,128)(2,1)S(1)}, bf16[1024,256]{1,0:T(8,128)(2,1)}, u32[]{:S(2)}) %copy-start.2) | copy-done | bytes 524312
  5.3 3.8 %shard_map.59.mine_ref = f32[512,1280]{1,0:T(8,128)S(1)} custom-call(s32[512]{0:T(512)S(1)} %constant_dynamic-update-slice_fusion.pivots_ref, bf16[1024,256]{1,0:T(8,128)(2,1)S(1)} %copy-done.2, f32[1024,1024]{1,0:T(8,128)S(1)} %copy-done), custom_call_target="tpu_custom_call" | custom-call | tf_op jit(solution)/shard_map/pallas_call | solution.py:61
  9.1 0.0 copy-start.1
  9.1 45.8 %shard_map.60 = f32[512,1280]{1,0:T(8,128)S(1)} custom-call(f32[512,1280]{1,0:T(8,128)S(1)} %shard_map.59.mine_ref), custom_call_target="tpu_custom_call" | custom-call | tf_op jit(solution)/shard_map/pallas_call | solution.py:179
  54.9 0.1 multiply_reduce_fusion.1
  55.1 0.0 copy-done.1
  55.1 0.0 copy-start.3
  55.1 5.0 %fusion.6 = f32[512,1024]{1,0:T(8,128)} fusion(f32[1024,1024]{1,0:T(8,128)S(1)} %copy-done.1, f32[512,1280]{1,0:T(8,128)S(1)} %shard_map.60), kind=kOutput, calls=%fused_computation.8 | convolution fusion | flops 3221225472 | bytes 8388608 | tf_op jit(solution)/shard_map/dot_general | solution.py:17
  60.1 0.0 copy-done.3
  60.1 0.2 multiply_reduce_fusion
  60.3 2.5 %bitcast_subtract_fusion = f32[1024,512]{0,1:T(8,128)S(1)} fusion(f32[512,1024]{1,0:T(8,128)} %fusion.6, bf16[1024,256]{1,0:T(8,128)(2,1)S(1)} %copy-done.3, s32[1024]{0:T(1024)S(1)} %iota_add_fusion, f32[512]{0:T(512)S(1)} %multiply_reduce_fusion.1, f32[1024]{0:T(1024)S(1)} %multiply_reduce_fusion, s32[512]{0:T(512)S(1)} %constant_dynamic-update-slice_fusion.pivots_ref, ...), kind=kOutput, calls=%fused_computation | convolution fusion | flops 273154048 | bytes 4993024 | tf_op jit(solution)/shard_map/dot_general | solution.py:17
  62.8 0.4 fusion.15
  63.2 1.9 %fusion.8.a_ref = f32[512,512]{1,0:T(8,128)S(1)} fusion(f32[512,512]{1,0:T(8,128)S(1)} %fusion.15, f32[512,1280]{1,0:T(8,128)S(1)} %shard_map.60), kind=kOutput, calls=%fused_computation.10 | convolution fusion | flops 1610874880 | bytes 4194304 | tf_op jit(solution)/shard_map/dot_general | solution.py:17
  65.1 22.0 %shard_map.61 = f32[512,512]{1,0:T(8,128)S(1)} custom-call(f32[512,512]{1,0:T(8,128)S(1)} %fusion.8.a_ref), custom_call_target="tpu_custom_call" | custom-call | tf_op jit(solution)/shard_map/pallas_call | solution.py:276
  87.2 2.8 %fusion.18 = f32[1024,256]{1,0:T(8,128)} fusion(f32[1024,512]{0,1:T(8,128)S(1)} %bitcast_subtract_fusion, f32[512,512]{1,0:T(8,128)S(1)} %shard_map.61), kind=kOutput, calls=%fused_computation.21 | convolution fusion | flops 805306368 | bytes 3670016 | tf_op jit(solution)/shard_map/dot_general | solution.py:17
  90.0 2.0 %fusion.16 = f32[1024,256]{1,0:T(8,128)} fusion(f32[1024,512]{0,1:T(8,128)S(1)} %bitcast_subtract_fusion, f32[512,512]{1,0:T(8,128)S(1)} %shard_map.61), kind=kOutput, calls=%fused_computation.17 | convolution fusion | flops 402653184 | bytes 2359296 | tf_op jit(solution)/shard_map/dot_general | solution.py:17
  (2 shorter events, 0.0 us)
Async XLA Ops:
  2.0 2.2 %copy-start = (f32[1024,1024]{1,0:T(8,128)S(1)}, f32[1024,1024]{1,0:T(8,128)}, u32[]{:S(2)}) copy-start(f32[1024,1024]{1,0:T(8,128)} %prior_ref.1) | copy-start | bytes 12582916
  4.2 1.0 %copy-start.2 = (bf16[1024,256]{1,0:T(8,128)(2,1)S(1)}, bf16[1024,256]{1,0:T(8,128)(2,1)}, u32[]{:S(2)}) copy-start(bf16[1024,256]{1,0:T(8,128)(2,1)} %points_ref.1) | copy-start | bytes 1572868
  9.1 46.0 %copy-start.1 = (f32[1024,1024]{1,0:T(8,128)S(1)}, f32[1024,1024]{1,0:T(8,128)}, u32[]{:S(2)}) copy-start(f32[1024,1024]{1,0:T(8,128)} %prior_ref.1) | copy-start | bytes 12582916
  55.1 5.0 %copy-start.3 = (bf16[1024,256]{1,0:T(8,128)(2,1)S(1)}, bf16[1024,256]{1,0:T(8,128)(2,1)}, u32[]{:S(2)}) copy-start(bf16[1024,256]{1,0:T(8,128)(2,1)} %points_ref.1) | copy-start | bytes 1572868
